TPU v7x, 32 devices: a whole 2x2x4 slice. The times are simulated.
32 devices in a mesh: freq: 4 (over y, core), trace: 8 (over z, x).
Axes of the slice: x: 2, y: 2, z: 4, core: 2. Of those that a mesh axis runs over, the one named last changes fastest.
Arguments:
- traces: bfloat16 [4, 2048, 4096], P('freq', 'trace'), may hold values from -6 to 6
- coords: int32 [4, 4, 2048], replicated, may hold values from 0 to 1023
- wavenumbers: int32 [4, 4, 4096], replicated, may hold values from 0 to 1023
- fold: int32 [4], replicated, may hold values from 256 to 2048, as said below
- selected: int32 [2, 4, 1024], P(None, None, 'freq'), may hold values from 0 to 4095
Outputs:
- spectrum: float32 [4096, 4, 2, 1024], P('trace', None, None, 'freq')
- coefficients: float32 [2, 4, 2, 1024], P(None, None, None, 'freq')
Inputs may be any that keep to these rules, and one draw needn't show every extreme that they name: Slots 0 to fold - 1 of a patch are live, the rest are not; some patch has all 2048 slots live.
All inputs are finite; a program needn't handle non-finite values.
Results may differ from a plain program's by a relative error of at most 0.0052.
Values may be sent and summed in bfloat16 or wider, within the bound.
A program may use at most 128 MiB of HBM per device.

v0:
```python
import math

import jax
import jax.numpy as jnp
from jax import lax
from jax.sharding import PartitionSpec as P

NF = 1024
NK = 4096
GRID = 1024
ITERS = 2


def dft_table(length, count):
    sample = jnp.arange(length, dtype=jnp.int32)
    bins = jnp.arange(count, dtype=jnp.int32)
    product = sample[:, None] * bins[None, :] % length
    angle = product.astype(jnp.float32) * (2.0 * math.pi / length)
    return jnp.concatenate([jnp.cos(angle), -jnp.sin(angle)], axis=1).astype(jnp.bfloat16)


def partial_spectrum(rows, places, wavenumbers, first_wave, wave_count):
    waves = lax.dynamic_slice_in_dim(wavenumbers, first_wave, wave_count, 2)
    inner = jnp.zeros((rows.shape[0], wave_count, rows.shape[1]), jnp.int32)
    for comp in range(4):
        inner = inner + waves[comp][:, :, None] * places[comp][:, None, :]
    inner = inner % GRID
    angle = inner.astype(jnp.float32) * (2.0 * math.pi / GRID)
    atoms = jnp.concatenate([jnp.cos(angle), jnp.sin(angle)], axis=1).astype(jnp.bfloat16)
    product = jnp.einsum("pks,psf->kpf", atoms, rows, preferred_element_type=jnp.float32)
    half = rows.shape[2] // 2
    s_real = product[:wave_count, :, :half] + product[wave_count:, :, half:]
    s_imag = product[:wave_count, :, half:] - product[wave_count:, :, :half]
    return jnp.stack([s_real, s_imag], axis=2)


def local(traces, coords, wavenumbers, fold, selected):
    slot_count = traces.shape[1]
    length = traces.shape[2]
    table = dft_table(length, NF)
    spectra = jnp.dot(traces.reshape(-1, length), table, preferred_element_type=jnp.float32)
    spectra = spectra.astype(jnp.bfloat16).reshape(traces.shape[0], slot_count, 2, NF)
    moved = lax.all_to_all(spectra, "freq", split_axis=3, concat_axis=0, tiled=True)
    patches = moved.shape[0]
    group_width = moved.shape[3]
    first_slot = lax.axis_index("trace") * slot_count
    my_coords = lax.dynamic_slice_in_dim(coords, first_slot, slot_count, 2)
    slot_index = first_slot + jnp.arange(slot_count, dtype=jnp.int32)
    live = (slot_index[None, :] < fold[:, None]).astype(jnp.float32)
    mask = live[:, :, None]
    res_real = moved[:, :, 0, :].astype(jnp.float32) * mask
    res_imag = moved[:, :, 1, :].astype(jnp.float32) * mask
    inverse = 1.0 / fold.astype(jnp.float32)
    gathered = []
    for iteration in range(ITERS):
        chosen = selected[iteration]
        picked = jnp.take_along_axis(
            wavenumbers, jnp.broadcast_to(chosen[None], (4,) + chosen.shape), axis=2
        )
        inner = jnp.zeros((patches, slot_count, group_width), jnp.int32)
        for comp in range(4):
            inner = inner + picked[comp][:, None, :] * my_coords[comp][:, :, None]
        inner = inner % GRID
        angle = inner.astype(jnp.float32) * (2.0 * math.pi / GRID)
        cosine = jnp.cos(angle)
        sine = jnp.sin(angle)
        part_real = jnp.sum(res_real * cosine + res_imag * sine, axis=1)
        part_imag = jnp.sum(res_imag * cosine - res_real * sine, axis=1)
        sum_real, sum_imag = lax.psum((part_real, part_imag), "trace")
        coef_real = sum_real * inverse[:, None]
        coef_imag = sum_imag * inverse[:, None]
        res_real = res_real - mask * (coef_real[:, None, :] * cosine - coef_imag[:, None, :] * sine)
        res_imag = res_imag - mask * (coef_real[:, None, :] * sine + coef_imag[:, None, :] * cosine)
        gathered.append(jnp.stack([coef_real, coef_imag], axis=1))
    rounded = jnp.concatenate([res_real, res_imag], axis=2).astype(jnp.bfloat16)
    wave_share = NK // lax.axis_size("trace")
    first_wave = lax.axis_index("trace") * wave_share
    spectrum = partial_spectrum(
        lax.all_gather(rounded, "trace", axis=1, tiled=True),
        coords,
        wavenumbers,
        first_wave,
        wave_share,
    )
    return (spectrum, jnp.stack(gathered, axis=0))


def solution(mesh):
    in_specs = (P("freq", "trace", None), P(), P(), P(), P(None, None, "freq"))
    out_specs = (P("trace", None, None, "freq"), P(None, None, None, "freq"))
    return jax.shard_map(local, mesh=mesh, in_specs=in_specs, out_specs=out_specs, check_vma=False)
```

profile of v0, /device:TPU:11, one launch (start us, length us, event | category | flops | bytes accessed | tf_op | source)
XLA Modules:
  0.0 417.5 jit_solution(6115092094940801331)
XLA Ops:
  7.2 0.0 copy-start
  7.2 68.7 %negate_convert_fusion = (bf16[4096,1024]{1,0:T(8,128)(2,1)}, bf16[4096,1024]{1,0:T(8,128)(2,1)}) fusion(), kind=kLoop, calls=%fused_computation.24 | loop fusion | flops 71303168 | bytes 16777216 | tf_op jit(solution)/shard_map/convert.7
  75.9 0.0 copy-done
  75.9 0.0 copy-start.4
  75.9 8.8 %fusion.20 = bf16[2048,256]{1,0:T(8,128)(2,1)S(1)} fusion(bf16[4096,1024]{1,0:T(8,128)(2,1)} %get-tuple-element.55, bf16[4096,1024]{1,0:T(8,128)(2,1)} %get-tuple-element.56, bf16[1,256,4096]{2,1,0:T(8,128)(2,1)S(1)} %copy-done), kind=kOutput, calls=%fused_computation.31 | convolution fusion | flops 4329046016 | bytes 19922944 | tf_op jit(solution)/shard_map/dot_general | solution.py:41
  84.7 0.0 copy-start.2
  84.7 2.0 copy.13
  86.7 4.2 all-to-all-start
  90.9 0.0 all-gather.2.cloned.1.call-start
  90.9 0.0 copy-done.4
  91.0 0.0 copy-done.2
  91.0 0.0 copy-start.5
  91.0 40.3 %gather_fusion = s32[4096]{0:T(1024)S(1)} fusion(s32[4,4,4096]{2,1,0:T(4,128)S(1)} %copy-done.2, s32[4096]{0:T(1024)S(1)} %bitcast.127), kind=kCustom, calls=%fused_computation.clone | custom fusion | bytes 81920 | tf_op jit(solution)/shard_map/jit(take_along_axis)/gather | solution.py:57
  131.3 0.0 copy-done.5
  131.4 0.1 compare_convert_fusion
  131.4 0.0 copy-start.3
  131.5 40.3 %gather_fusion.1 = s32[4096]{0:T(1024)S(1)} fusion(s32[4,4,4096]{2,1,0:T(4,128)S(1)} %copy-done.2, s32[4096]{0:T(1024)S(1)} %bitcast.128), kind=kCustom, calls=%fused_computation.1.clone | custom fusion | bytes 81920 | tf_op jit(solution)/shard_map/jit(take_along_axis)/gather | solution.py:57
  171.8 0.0 copy-done.3
  171.9 0.0 all-to-all-done
  171.9 0.1 copy.14
  172.0 5.5 %fusion.36 = (f32[4,256]{1,0:T(4,128)S(1)}, f32[4,256]{1,0:T(4,128)S(1)}) fusion(s32[4,256]{1,0:T(4,128)S(1)} %get-tuple-element.34, s32[4,256]{1,0:T(4,128)S(1)} %get-tuple-element.36, s32[4,256]{1,0:T(4,128)S(1)} %get-tuple-element.32, s32[4,256]{1,0:T(4,128)S(1)} %get-tuple-element.37, s32[4,256]{1,0:T(4,128)S(1)} %get-tuple-element.33, ...), kind=kLoop, calls=%fused_computation.55 | loop fusion | flops 8386560 | bytes 1093632 | tf_op jit(solution)/shard_map/reduce_sum | solution.py:67
  177.5 12.1 %all-reduce.1 = (f32[4,256]{1,0:T(4,128)S(1)}, f32[4,256]{1,0:T(4,128)S(1)}) all-reduce(f32[4,256]{1,0:T(4,128)S(1)} %get-tuple-element.12, f32[4,256]{1,0:T(4,128)S(1)} %get-tuple-element.11), channel_id=1, replica_groups=mesh['freq'=4,'trace'=8] {'trace'}, use_global_device_ids=true, to_apply=%region_3.5 | all-reduce | flops 2048 | bytes 16384 | tf_op jit(solution)/shard_map/psum | solution.py:69
  189.6 0.1 broadcast_multiply_fusion.3
  189.7 13.9 %add_reduce_fusion = (f32[4,256]{1,0:T(4,128)S(1)}, f32[4,256]{1,0:T(4,128)S(1)}) fusion(s32[4,256]{1,0:T(4,128)S(1)} %get-tuple-element.34, s32[4,256]{1,0:T(4,128)S(1)} %get-tuple-element.40, s32[4,256]{1,0:T(4,128)S(1)} %get-tuple-element.32, s32[4,256]{1,0:T(4,128)S(1)} %get-tuple-element.41, s32[4,256]{1,0:T(4,128)S(1)} %get-tuple-element.33, ...), kind=kLoop, calls=%fused_computation.65 | loop fusion | flops 16250880 | bytes 1118208 | tf_op jit(solution)/shard_map/reduce_sum | solution.py:67
  203.6 17.6 %all-reduce = (f32[4,256]{1,0:T(4,128)S(1)}, f32[4,256]{1,0:T(4,128)S(1)}) all-reduce(f32[4,256]{1,0:T(4,128)S(1)} %get-tuple-element.10, f32[4,256]{1,0:T(4,128)S(1)} %get-tuple-element.9), channel_id=1, replica_groups=mesh['freq'=4,'trace'=8] {'trace'}, use_global_device_ids=true, to_apply=%region_7.9 | all-reduce | flops 2048 | bytes 16384 | tf_op jit(solution)/shard_map/psum | solution.py:69
  221.1 0.1 broadcast_multiply_fusion.1
  221.2 27.8 %subtract_convert_fusion.1 = (bf16[4,256,256]{1,2,0:T(8,128)(2,1)S(1)}, bf16[4,256,256]{1,2,0:T(8,128)(2,1)S(1)}) fusion(f32[4,256]{1,0:T(4,128)S(1)} %get-tuple-element.50, f32[4,256]{1,0:T(4,128)S(1)} %get-tuple-element.49, s32[4,256]{1,0:T(4,128)S(1)} %get-tuple-element.34, s32[4,256]{1,0:T(4,128)S(1)} %get-tuple-element.40, ...), kind=kLoop, calls=%fused_computation.63 | loop fusion | flops 17301504 | bytes 2166784 | tf_op jit(solution)/shard_map/convert.4
  249.0 1.0 pad_maximum_fusion.1
  250.0 0.0 all-gather.2.cloned.1.call-update
  250.1 73.0 %cosine_convert_fusion = (bf16[4,512,2048]{2,1,0:T(8,128)(2,1)}, bf16[4,512,2048]{2,1,0:T(8,128)(2,1)}) fusion(s32[4,2048]{1,0:T(4,128)S(1)} %get-tuple-element.29, s32[4,512]{1,0:T(4,128)S(1)} %get-tuple-element.24, s32[4,2048]{1,0:T(4,128)S(1)} %get-tuple-element.30, s32[4,512]{1,0:T(4,128)S(1)} %get-tuple-element.22, s32[4,2048]{1,0:T(4,128)S(1)} %get-tuple-element.28, ...), kind=kLoop, calls=%fused_computation.23 | loop fusion | flops 92274688 | bytes 16941056 | tf_op jit(solution)/shard_map/convert.2
  323.2 0.6 pad_maximum_fusion.2
  323.8 57.0 %all-gather.2.cloned.1.call-done = bf16[4,2048,512]{1,2,0:T(8,128)(2,1)} async-done(((bf16[4,256,512]{1,2,0:T(8,128)(2,1)}), bf16[4,2048,512]{1,2,0:T(8,128)(2,1)}) %all-gather.2.cloned.1.call-update) | async-done | bytes 8388624 | tf_op jit(solution)/shard_map/all_gather | solution.py:79
  380.7 15.7 %fusion.17 = f32[1024,4,512]{0,2,1:T(8,128)} fusion(bf16[4,2048,512]{1,2,0:T(8,128)(2,1)} %all-gather.2.cloned.1.call-done, bf16[4,512,2048]{2,1,0:T(8,128)(2,1)} %get-tuple-element.26, bf16[4,512,2048]{2,1,0:T(8,128)(2,1)} %get-tuple-element.25), kind=kOutput, calls=%fused_computation.30 | convolution fusion | flops 8623489024 | bytes 33554432 | tf_op jit(solution)/shard_map/pks,psf->kpf/dot_general | solution.py:30
  396.4 4.5 %fusion.24 = (f32[512,4,1,256]{0,3,1,2:T(8,128)S(1)}, f32[512,4,1,256]{0,3,1,2:T(8,128)S(1)}) fusion(f32[1024,4,512]{0,2,1:T(8,128)} %fusion.17), kind=kLoop, calls=%fused_computation.35 | loop fusion | flops 1048576 | bytes 12582912 | tf_op jit(solution)/shard_map/stack | solution.py:34
  400.9 0.0 copy-start.1
  401.0 2.4 pad_maximum_fusion
  403.3 7.3 %copy.17 = f32[512,4,2,256]{3,2,1,0:T(2,128)} copy(f32[512,4,2,256]{0,3,1,2:T(8,128)} %pad_maximum_fusion) | data formatting | bytes 8388608
  410.6 0.0 copy-done.1
  (22 shorter events, 0.2 us)
Async XLA Ops:
  7.2 68.7 %copy-start = (bf16[1,256,4096]{2,1,0:T(8,128)(2,1)S(1)}, bf16[1,256,4096]{2,1,0:T(8,128)(2,1)}, u32[]{:S(2)}) copy-start(bf16[1,256,4096]{2,1,0:T(8,128)(2,1)} %param.7) | copy-start | bytes 6291460
  75.9 15.0 %copy-start.4 = (s32[2,4,256]{2,1,0:T(4,128)S(1)}, s32[2,4,256]{2,1,0:T(4,128)}, u32[]{:S(2)}) copy-start(s32[2,4,256]{2,1,0:T(4,128)} %param.11) | copy-start | bytes 24580
  84.7 6.3 %copy-start.2 = (s32[4,4,4096]{2,1,0:T(4,128)S(1)}, s32[4,4,4096]{2,1,0:T(4,128)}, u32[]{:S(2)}) copy-start(s32[4,4,4096]{2,1,0:T(4,128)} %param.9) | copy-start | bytes 786436
  86.7 85.2 %all-to-all-start = ((bf16[1,256,2,1024]{1,2,0,3:T(2,128)(2,1)}), bf16[1,256,2,1024]{1,2,0,3:T(2,128)(2,1)S(1)}, u32[]{:S(2)}, u32[]{:S(2)}) async-start(bf16[1,256,2,1024]{1,2,0,3:T(2,128)(2,1)} %copy.13), calls=%async_computation | async-start | bytes 2097152 | tf_op jit(solution)/shard_map/all_to_all | solution.py:43
  90.9 289.9 %all-gather.2.cloned.1.call-start = ((), (), s32[]{:S(2)}) async-start(), calls=%async_computation.1 | async-start | bytes 9437184 | tf_op jit(solution)/shard_map/all_gather | solution.py:79
  91.0 40.4 %copy-start.5 = (s32[4]{0:T(128)S(1)}, s32[4]{0:T(128)}, u32[]{:S(2)}) copy-start(s32[4]{0:T(128)} %param.10) | copy-start | bytes 52
  131.4 40.3 %copy-start.3 = (s32[4,4,2048]{2,1,0:T(4,128)S(1)}, s32[4,4,2048]{2,1,0:T(4,128)}, u32[]{:S(2)}) copy-start(s32[4,4,2048]{2,1,0:T(4,128)} %param.8) | copy-start | bytes 393220
  400.9 9.7 %copy-start.1 = (bf16[1,256,4096]{2,1,0:T(8,128)(2,1)S(1)}, bf16[1,256,4096]{2,1,0:T(8,128)(2,1)}, u32[]{:S(2)}) copy-start(bf16[1,256,4096]{2,1,0:T(8,128)(2,1)} %param.7) | copy-start | bytes 6291460
Sparse Core Ops, SparseCore 0:
  250.2 130.5 all-gather.1
where the time goes:
time: 423 us; the launch traced here: 417 us
  other arithmetic  198 us (47%)
  local copies, waits for them, and re-layouts  90.2 us (21%)
  waiting for transfers between devices  57 us (13%)
  blocking collectives  29.7 us (7%)
  matrix products  24.4 us (6%)
  between operations  14.3 us (3%)
    another operation x3, other arithmetic  169 us
    gather x4, local copies, waits for them, and re-layouts, local(): jnp.take_along_axis(wavenumbers, jnp.broadcast_to(chosen[None], (4,) + ch...  80.6 us
    all_gather x1, waiting for transfers between devices, local(): lax.all_gather(rounded, 'trace', axis=1, tiled=True)  57 us
    psum x2, blocking collectives, local(): sum_real, sum_imag = lax.psum((part_real, part_imag), 'trace')  29.7 us
    reduce_sum x2, other arithmetic, local(): part_real = jnp.sum(res_real * cosine + res_imag * sine, axis=1)  19.4 us
    dot_general x1, matrix products, partial_spectrum(): jnp.einsum('pks,psf->kpf', atoms, rows, preferred_element_type=jnp.float32)  15.7 us
    dot_general x1, matrix products, local(): jnp.dot(traces.reshape(-1, length), table, preferred_element_type=jnp.flo...  8.76 us
  transfers between devices with their start and end apart: 2, of which 1 were waited for; matrix products, arithmetic and copies ran while one was open for 37% of the time, Pallas kernels for 0%

commit v1 on v0

v1 whole, which is shorter than its diff:
```python
import functools
import math

import jax
import jax.numpy as jnp
import ml_dtypes
import numpy as np
from jax import lax
from jax.experimental import pallas as pl
from jax.experimental.pallas import tpu as pltpu
from jax.sharding import PartitionSpec as P

NF = 1024
DIGIT = 32
ITERS = 2
PRE = 4
MESH = pl.DeviceIdType.MESH

SIN_ATOM = (6.2830558, -41.33121428, 81.36681487, -74.47800194, 32.78139554)
COS_ATOM = (0.9999598, -19.73104175, 64.6734317, -82.40355228, 45.64655792)
SIN_FINE = (6.28318527, -41.34169707, 81.60502462, -76.70155117, 42.01616576, -14.86861079, 3.19969338)
COS_FINE = (0.99999999, -19.73920453, 64.93911899, -85.45016556, 60.16783179, -25.96831339, 6.52961042)


def horner(u, coefs):
    acc = u * coefs[-1] + coefs[-2]
    for c in coefs[-3::-1]:
        acc = acc * u + c
    return acc


def turn(x, sin_coefs, cos_coefs):
    x = x - jnp.round(x)
    u = x * x
    return horner(u, cos_coefs), horner(u, sin_coefs) * x


def dft_blocks(length, blocks):
    sample = np.arange(length, dtype=np.int64)
    bins = np.arange(NF, dtype=np.int64)
    angle = (sample[:, None] * bins[None, :] % length) * (2.0 * math.pi / length)
    pair = np.stack([np.cos(angle), -np.sin(angle)], axis=1).astype(np.float32)
    width = NF // blocks
    pair = pair.reshape(length, 2, blocks, width).transpose(2, 0, 1, 3)
    return pair.reshape(blocks, length, 2 * width).astype(ml_dtypes.bfloat16)


def kernel(n_freq, n_trace, traces, table, wd, cd, cdt, kd, live, inv, recv, coef_out,
           tab, spec, spread, osc, res, atoms, obuf, coef_my,
           tab_sem, s_send, s_recv, s_loc, c_send, c_recv, o_send, o_recv, o_loc):
    halves = n_trace // n_freq
    g = lax.axis_index("freq")
    t = lax.axis_index("trace")
    own_patch = t // halves
    slots = spread.shape[1]
    total = n_trace * slots
    fb = osc.shape[2]
    share = obuf.shape[1]
    n_buf = atoms.shape[0]
    pre = n_buf - 1

    def table_copy(j):
        block = lax.rem(j + t, n_trace)
        return pltpu.make_async_copy(table.at[block], tab.at[lax.rem(j, 2)], tab_sem.at[lax.rem(j, 2)])

    table_copy(0).start()

    barrier = pltpu.get_barrier_semaphore()

    @pl.loop(0, n_trace)
    def _(k):
        @pl.when(jnp.logical_or(own_patch != g, k != t))
        def _():
            pl.semaphore_signal(barrier, inc=1, device_id=(own_patch, k), device_id_type=MESH)

        @pl.when(k != t)
        def _():
            pl.semaphore_signal(barrier, inc=1, device_id=(g, k), device_id_type=MESH)

    pl.semaphore_wait(barrier, 2 * n_trace - 1 - (own_patch == g).astype(jnp.int32))

    def spec_copy(j):
        block = lax.rem(j + t, n_trace)
        to_freq, to_trace = block // halves, g * halves + lax.rem(block, halves)
        return to_freq, to_trace, pltpu.make_async_remote_copy(
            src_ref=spec.at[j], dst_ref=spread.at[t], send_sem=s_send.at[j], recv_sem=s_recv.at[t],
            device_id=(to_freq, to_trace), device_id_type=MESH)

    def self_copy(j):
        return pltpu.make_async_copy(spec.at[j], spread.at[t], s_loc)

    @pl.loop(0, n_trace)
    def _(j):
        @pl.when(j + 1 < n_trace)
        def _():
            table_copy(j + 1).start()

        table_copy(j).wait()
        spec[j] = jnp.dot(traces[...], tab[lax.rem(j, 2)], preferred_element_type=jnp.float32).astype(jnp.bfloat16)
        to_freq, to_trace, copy = spec_copy(j)
        mine = jnp.logical_and(to_freq == g, to_trace == t)

        @pl.when(mine)
        def _():
            self_copy(j).start()

        @pl.when(jnp.logical_not(mine))
        def _():
            copy.start()

    rows = min(256, share)
    lanes = 256

    def make_atoms(i):
        base = lax.rem(t + 1 + i, n_trace) * share
        buf = lax.rem(i, n_buf)

        @pl.loop(0, (share // rows) * (total // lanes))
        def _(q):
            r = pl.multiple_of((q // (total // lanes)) * rows, rows)
            c = pl.multiple_of(lax.rem(q, total // lanes) * lanes, lanes)
            x = jnp.dot(wd[pl.ds(base + r, rows), :], cd[:, pl.ds(c, lanes)], preferred_element_type=jnp.float32)
            cosine, sine = turn(x, SIN_ATOM, COS_ATOM)
            atoms[buf, pl.ds(r, rows), pl.ds(c, lanes)] = cosine.astype(jnp.bfloat16)
            atoms[buf, pl.ds(r, rows), pl.ds(total + c, lanes)] = sine.astype(jnp.bfloat16)

    @pl.loop(0, n_trace)
    def _(k):
        at = pl.ds(pl.multiple_of(k * slots, slots), slots)
        on = live[at, :]
        for it in range(ITERS):
            x = jnp.dot(cdt[at, :], kd[it], preferred_element_type=jnp.float32)
            cosine, sine = turn(x, SIN_FINE, COS_FINE)
            osc[2 * it, at, :] = cosine * on
            osc[2 * it + 1, at, :] = sine * on

    @pl.loop(0, pre)
    def _(i):
        make_atoms(i)

    def fold8(a):
        return jnp.sum(a.reshape(a.shape[0] // 8, 8, fb), axis=0)

    def add_block(k, sums):
        own = jnp.logical_and(own_patch == g, k == t)

        @pl.when(own)
        def _():
            pltpu.make_async_copy(spec.at[0], spread.at[k], s_loc).wait()

        @pl.when(jnp.logical_not(own))
        def _():
            pltpu.make_async_remote_copy(
                src_ref=spec.at[0], dst_ref=spread.at[k], send_sem=s_send.at[0], recv_sem=s_recv.at[k],
                device_id=(own_patch, k), device_id_type=MESH).wait_recv()

        at = pl.ds(pl.multiple_of(k * slots, slots), slots)
        x = spread[k].astype(jnp.float32)
        re, im = x[:, :fb], x[:, fb:]
        c1, s1, c2, s2 = (osc[n, at, :] for n in range(4))
        terms = (re * c1 + im * s1, im * c1 - re * s1, re * c2 + im * s2, im * c2 - re * s2,
                 c1 * c2 + s1 * s2, s1 * c2 - c1 * s2)
        return tuple(a + fold8(b) for a, b in zip(sums, terms))

    zero = jnp.zeros((8, fb), jnp.float32)
    sums = lax.fori_loop(0, n_trace, add_block, (zero,) * 6)
    p1r, p1i, p2r, p2i, gr, gi = (jnp.sum(a, axis=0, keepdims=True) for a in sums)
    scale = inv[...]
    a1r, a1i = p1r * scale, p1i * scale
    a2r = (p2r - (a1r * gr - a1i * gi)) * scale
    a2i = (p2i - (a1r * gi + a1i * gr)) * scale
    coef_my[...] = jnp.zeros_like(coef_my)
    for n, a in enumerate((a1r, a1i, a2r, a2i)):
        coef_my[n : n + 1, :] = a

    def coef_copy(k):
        return pltpu.make_async_remote_copy(
            src_ref=coef_my, dst_ref=coef_out.at[t], send_sem=c_send.at[k], recv_sem=c_recv.at[t],
            device_id=(g, k), device_id_type=MESH)

    @pl.loop(0, n_trace)
    def _(k):
        @pl.when(k != t)
        def _():
            coef_copy(k).start()

        @pl.when(k == t)
        def _():
            coef_out[t] = coef_my[...]

    @pl.loop(0, n_trace)
    def _(k):
        at = pl.ds(pl.multiple_of(k * slots, slots), slots)
        under = pl.ds(pl.multiple_of(total + k * slots, slots), slots)
        on = live[at, :]
        x = spread[k].astype(jnp.float32)
        c1, s1, c2, s2 = (osc[n, at, :] for n in range(4))
        re = x[:, :fb] * on - (a1r * c1 - a1i * s1) - (a2r * c2 - a2i * s2)
        im = x[:, fb:] * on - (a1r * s1 + a1i * c1) - (a2r * s2 + a2i * c2)
        res[at, :fb] = re.astype(jnp.bfloat16)
        res[at, fb:] = im.astype(jnp.bfloat16)
        res[under, :fb] = im.astype(jnp.bfloat16)
        res[under, fb:] = (-re).astype(jnp.bfloat16)

    def out_copy(i):
        return pltpu.make_async_remote_copy(
            src_ref=obuf.at[i], dst_ref=recv.at[t], send_sem=o_send.at[i], recv_sem=o_recv.at[t],
            device_id=(g, lax.rem(t + 1 + i, n_trace)), device_id_type=MESH)

    @pl.loop(0, n_trace)
    def _(i):
        buf = lax.rem(i, n_buf)

        @pl.loop(0, share // rows)
        def _(r):
            at = pl.ds(pl.multiple_of(r * rows, rows), rows)
            obuf[i, at, :] = jnp.dot(atoms[buf, at, :], res[...], preferred_element_type=jnp.float32).astype(jnp.bfloat16)

        @pl.when(i < n_trace - 1)
        def _():
            out_copy(i).start()

        @pl.when(i + pre < n_trace)
        def _():
            make_atoms(i + pre)

    own_out = pltpu.make_async_copy(obuf.at[n_trace - 1], recv.at[t], o_loc)
    own_out.start()

    @pl.loop(0, n_trace)
    def _(j):
        to_freq, to_trace, copy = spec_copy(j)

        @pl.when(jnp.logical_not(jnp.logical_and(to_freq == g, to_trace == t)))
        def _():
            copy.wait_send()

        @pl.when(j != t)
        def _():
            coef_copy(j).wait_send()
            pltpu.make_async_remote_copy(
                src_ref=coef_my, dst_ref=coef_out.at[j], send_sem=c_send.at[j], recv_sem=c_recv.at[j],
                device_id=(g, j), device_id_type=MESH).wait_recv()
            pltpu.make_async_remote_copy(
                src_ref=obuf.at[0], dst_ref=recv.at[j], send_sem=o_send.at[0], recv_sem=o_recv.at[j],
                device_id=(g, j), device_id_type=MESH).wait_recv()

        @pl.when(j < n_trace - 1)
        def _():
            out_copy(j).wait_send()

    own_out.wait()


def digits_low(v):
    a, b = v // DIGIT, v % DIGIT
    rows = jnp.concatenate([a * DIGIT, b * DIGIT, b], axis=0).astype(jnp.float32) / (DIGIT * DIGIT)
    return jnp.pad(rows, ((0, 4), (0, 0))).astype(jnp.bfloat16)


def digits_high(v):
    d, e = v // DIGIT, v % DIGIT
    rows = jnp.concatenate([e, d, e], axis=0)
    return jnp.pad(rows, ((0, 4), (0, 0))).astype(jnp.bfloat16)


def local(traces, coords, wavenumbers, fold, selected):
    slots, length = traces.shape[1:]
    n_freq, n_trace = lax.axis_size("freq"), lax.axis_size("trace")
    patches = coords.shape[1]
    halves = n_trace // n_freq
    fb = NF // n_trace
    n_waves = wavenumbers.shape[2]
    share = n_waves // n_trace
    total = coords.shape[2]
    t = lax.axis_index("trace")
    patch = t // halves
    table = jnp.asarray(dft_blocks(length, n_trace))
    waves = digits_low(lax.dynamic_index_in_dim(wavenumbers, patch, 1, keepdims=False))
    places = digits_high(lax.dynamic_index_in_dim(coords, patch, 1, keepdims=False))
    chosen = lax.dynamic_slice(selected, (0, patch, lax.rem(t, halves) * fb), (ITERS, 1, fb)).reshape(-1)
    onehot = (jnp.arange(n_waves, dtype=jnp.int32)[:, None] == chosen[None, :]).astype(jnp.bfloat16)
    picked = jnp.dot(waves, onehot, preferred_element_type=jnp.float32).astype(jnp.bfloat16)
    kd = picked.reshape(16, ITERS, fb).transpose(1, 0, 2)
    my_fold = lax.dynamic_index_in_dim(fold, patch, 0, keepdims=False)
    live = (jnp.arange(total, dtype=jnp.int32) < my_fold).astype(jnp.float32)
    live = jnp.broadcast_to(live[:, None], (total, fb))
    inv = jnp.broadcast_to(1.0 / my_fold.astype(jnp.float32), (1, fb))
    vmem = pl.BlockSpec(memory_space=pltpu.VMEM)
    hbm = pl.BlockSpec(memory_space=pl.ANY)
    dma = pltpu.SemaphoreType.DMA
    n_buf = min(PRE, n_trace - 1) + 1
    bf16, f32 = jnp.bfloat16, jnp.float32
    recv, coef = pl.pallas_call(
        functools.partial(kernel, n_freq, n_trace),
        out_shape=(jax.ShapeDtypeStruct((n_trace, share, 2 * fb), bf16),
                   jax.ShapeDtypeStruct((n_trace, 8, fb), f32)),
        in_specs=[vmem, hbm, vmem, vmem, vmem, vmem, vmem, vmem],
        out_specs=(hbm, vmem),
        scratch_shapes=[
            pltpu.VMEM((2, length, 2 * fb), bf16),
            pltpu.VMEM((n_trace, slots, 2 * fb), bf16),
            pltpu.VMEM((n_trace, slots, 2 * fb), bf16),
            pltpu.VMEM((2 * ITERS, total, fb), f32),
            pltpu.VMEM((2 * total, 2 * fb), bf16),
            pltpu.VMEM((n_buf, share, 2 * total), bf16),
            pltpu.VMEM((n_trace, share, 2 * fb), bf16),
            pltpu.VMEM((8, fb), f32),
            dma((2,)), dma((n_trace,)), dma((n_trace,)), dma,
            dma((n_trace,)), dma((n_trace,)), dma((n_trace,)), dma((n_trace,)), dma,
        ],
        compiler_params=pltpu.CompilerParams(
            collective_id=0, has_side_effects=True, vmem_limit_bytes=58 * 1024 * 1024),
    )(traces[0], table, waves.T, places, places.T, kd, live, inv)
    spectrum = recv.reshape(patches, halves, share, 2, fb).transpose(2, 0, 3, 1, 4)
    spectrum = spectrum.reshape(share, patches, 2, halves * fb).astype(f32)
    coef = coef[:, : 2 * ITERS].reshape(patches, halves, ITERS, 2, fb).transpose(2, 0, 3, 1, 4)
    return spectrum, coef.reshape(ITERS, patches, 2, halves * fb)


def solution(mesh):
    in_specs = (P("freq", "trace", None), P(), P(), P(), P(None, None, "freq"))
    out_specs = (P("trace", None, None, "freq"), P(None, None, None, "freq"))
    return jax.shard_map(local, mesh=mesh, in_specs=in_specs, out_specs=out_specs, check_vma=False)
```

time: 423 us -> 150 us (0.35); the launches traced: 417 us -> 149 us
  other arithmetic: 198 us -> 0.96 us
  Pallas kernels: 0 us -> 115 us
  local copies, waits for them, and re-layouts: 90.2 us -> 30.7 us
  waiting for transfers between devices: 57 us -> 0 us
  blocking collectives: 29.7 us -> 0 us
  matrix products: 24.4 us -> 0.96 us
  between operations: 14.3 us -> 1.42 us
    another operation x8 -> x2, other arithmetic: 177 us -> 0.14 us
    pallas_call x0 -> x1, Pallas kernels: none -> 115 us  [local(): pl.pallas_call(functools.partial(kernel, n_freq, n_trace), out_shape=(jax...]
    gather x4 -> x0, local copies, waits for them, and re-layouts: 80.6 us -> none  [local(): jnp.take_along_axis(wavenumbers, jnp.broadcast_to(chosen[None], (4,) + ch...]
    all_gather x1 -> x0, waiting for transfers between devices: 57 us -> none  [local(): lax.all_gather(rounded, 'trace', axis=1, tiled=True)]
    psum x2 -> x0, blocking collectives: 29.7 us -> none  [local(): sum_real, sum_imag = lax.psum((part_real, part_imag), 'trace')]
    dot_general x2 -> x1, matrix products: 24.4 us -> 0.96 us  [local(): jnp.dot(waves, onehot, preferred_element_type=jnp.float32)]
    convert_element_type x0 -> x3, local copies, waits for them, and re-layouts: none -> 20 us  [local(): spectrum = spectrum.reshape(share, patches, 2, halves * fb).astype(f32)]
    reduce_sum x2 -> x0, other arithmetic: 19.4 us -> none  [local(): part_real = jnp.sum(res_real * cosine + res_imag * sine, axis=1)]
  transfers between devices with their start and end apart: 2 -> 0, of which waited for: 1 -> 0; matrix products, arithmetic and copies ran while one was open for 37% -> 0% of each run, Pallas kernels for 0% -> 0%
where the time goes in v1:
time: 150 us; the launch traced here: 149 us
  Pallas kernels  115 us (77%)
  local copies, waits for them, and re-layouts  30.7 us (20%)
    pallas_call x1, Pallas kernels, local(): pl.pallas_call(functools.partial(kernel, n_freq, n_trace), out_shape=(jax...  115 us
    convert_element_type x3, local copies, waits for them, and re-layouts, local(): spectrum = spectrum.reshape(share, patches, 2, halves * fb).astype(f32)  20 us

profile of v1, /device:TPU:11, one launch (start us, length us, event | category | flops | bytes accessed | tf_op | source)
XLA Modules:
  0.0 149.1 jit_solution(3222505019668681695)
XLA Ops:
  0.6 0.0 copy-start
  0.7 1.3 dynamic_slice.18
  2.6 0.6 broadcast_in_dim.5.inv
  3.2 0.8 constant_dynamic-slice_fusion
  4.0 0.6 fusion.14
  4.6 0.9 constant_dynamic-slice_fusion.1
  5.6 0.1 fusion.11
  5.7 0.0 copy-done
  5.7 0.1 constant_dynamic-slice_fusion.2
  5.8 0.1 broadcast_multiply_fusion
  6.0 0.1 fusion.6
  6.0 0.3 copy.34
  6.3 0.2 copy.73
  6.5 0.9 pad_bitcast_fusion.1.cdt
  7.5 0.6 pad.11.clone.cd
  8.1 0.5 copy.33
  8.6 1.0 fusion.3
  9.5 1.2 pad_bitcast_fusion.wd
  10.7 0.6 copy.75
  11.3 1.3 broadcast_in_dim.4.live
  12.6 115.0 %shard_map.77 = (bf16[8,512,256]{2,1,0:T(8,128)(2,1)}, f32[8,8,128]{2,1,0:T(8,128)}) custom-call(bf16[256,4096]{1,0:T(8,128)(2,1)} %bitcast.65, bf16[8,4096,256]{2,1,0:T(8,128)(2,1)} %constant.91.clone.table, bf16[4096,16]{1,0:T(8,128)(2,1)} %pad_bitcast_fusion.wd, bf16[16,2048]{1,0:T(8,128)(2,1)} %pad.11.clone.cd, bf16[2048,16]{1,0:T(8,128)(2,1)} %pad_bitcast_fusion.1.cdt, ...), custom_call_target="tpu_custom_call" | custom-call | tf_op jit(solution)/shard_map/pallas_call | solution.py:294
  127.7 0.8 slice.3
  128.5 0.6 reshape.27
  129.1 5.1 %reshape.29 = f32[4,2,512,2,128]{4,3,2,1,0:T(2,128)} reshape(bf16[8,512,256]{2,1,0:T(8,128)(2,1)} %get-tuple-element.4) | data formatting | bytes 6291456 | tf_op jit(solution)/shard_map/convert_element_type | solution.py:316
  134.2 7.4 %copy.37 = f32[512,4,2,2,128]{4,3,2,1,0:T(2,128)} copy(f32[512,4,2,2,128]{4,2,0,3,1:T(2,128)} %bitcast.64) | data formatting | bytes 8388608 | tf_op jit(solution)/shard_map/convert_element_type | solution.py:316
  141.5 7.5 %reshape.28 = f32[512,4,2,256]{3,2,1,0:T(2,128)} reshape(f32[512,4,2,2,128]{4,3,2,1,0:T(2,128)} %copy.37) | data formatting | bytes 8388608 | tf_op jit(solution)/shard_map/convert_element_type | solution.py:316
  (2 shorter events, 0.0 us)
Async XLA Ops:
  0.6 5.1 %copy-start = (s32[4,4,4096]{2,1,0:T(4,128)S(1)}, s32[4,4,4096]{2,1,0:T(4,128)}, u32[]{:S(2)}) copy-start(s32[4,4,4096]{2,1,0:T(4,128)} %param.8) | copy-start | bytes 786436

commit v2 on v1

--- a/solution.py
+++ b/solution.py
@@ -51,7 +51,7 @@
     halves = n_trace // n_freq
     g = lax.axis_index("freq")
     t = lax.axis_index("trace")
-    own_patch = t // halves
+    own_patch = lax.rem(t // halves + g, n_freq)
     slots = spread.shape[1]
     total = n_trace * slots
     fb = osc.shape[2]
@@ -81,7 +81,8 @@
 
     def spec_copy(j):
         block = lax.rem(j + t, n_trace)
-        to_freq, to_trace = block // halves, g * halves + lax.rem(block, halves)
+        to_freq = block // halves
+        to_trace = lax.rem(g + n_freq - to_freq, n_freq) * halves + lax.rem(block, halves)
         return to_freq, to_trace, pltpu.make_async_remote_copy(
             src_ref=spec.at[j], dst_ref=spread.at[t], send_sem=s_send.at[j], recv_sem=s_recv.at[t],
             device_id=(to_freq, to_trace), device_id_type=MESH)
@@ -252,6 +253,24 @@
     own_out.wait()
 
 
+def unpack(patches, recv, out):
+    n_trace, step, _ = recv.shape
+    halves = n_trace // patches
+    fb = recv.shape[2] // 2
+    row = out.shape[1]
+    blocks = halves * fb // row
+    stride = patches * blocks * 2
+    g = lax.axis_index("freq")
+    for p in range(patches):
+        at = lax.rem(p + patches - g, patches) * halves
+        parts = [recv[at + h].astype(jnp.float32) for h in range(halves)]
+        for ri in range(2):
+            full = jnp.concatenate([a[:, ri * fb : (ri + 1) * fb] for a in parts], axis=1)
+            for b in range(blocks):
+                first = (p * blocks + b) * 2 + ri
+                out[pl.ds(first, step, stride=stride), :] = full[:, b * row : (b + 1) * row]
+
+
 def digits_low(v):
     a, b = v // DIGIT, v % DIGIT
     rows = jnp.concatenate([a * DIGIT, b * DIGIT, b], axis=0).astype(jnp.float32) / (DIGIT * DIGIT)
@@ -274,7 +293,7 @@
     share = n_waves // n_trace
     total = coords.shape[2]
     t = lax.axis_index("trace")
-    patch = t // halves
+    patch = lax.rem(t // halves + lax.axis_index("freq"), patches)
     table = jnp.asarray(dft_blocks(length, n_trace))
     waves = digits_low(lax.dynamic_index_in_dim(wavenumbers, patch, 1, keepdims=False))
     places = digits_high(lax.dynamic_index_in_dim(coords, patch, 1, keepdims=False))
@@ -312,10 +331,22 @@
         compiler_params=pltpu.CompilerParams(
             collective_id=0, has_side_effects=True, vmem_limit_bytes=58 * 1024 * 1024),
     )(traces[0], table, waves.T, places, places.T, kd, live, inv)
-    spectrum = recv.reshape(patches, halves, share, 2, fb).transpose(2, 0, 3, 1, 4)
-    spectrum = spectrum.reshape(share, patches, 2, halves * fb).astype(f32)
-    coef = coef[:, : 2 * ITERS].reshape(patches, halves, ITERS, 2, fb).transpose(2, 0, 3, 1, 4)
-    return spectrum, coef.reshape(ITERS, patches, 2, halves * fb)
+    width = halves * fb
+    row = min(width, 128)
+    step = min(share, 128)
+    rows = patches * 2 * (width // row)
+    spectrum = pl.pallas_call(
+        functools.partial(unpack, patches),
+        out_shape=jax.ShapeDtypeStruct((share * rows, row), f32),
+        grid=(share // step,),
+        in_specs=[pl.BlockSpec((n_trace, step, 2 * fb), lambda i: (0, i, 0))],
+        out_specs=pl.BlockSpec((step * rows, row), lambda i: (i, 0)),
+    )(recv)
+    spectrum = spectrum.reshape(share, patches, width // row, 2, row).transpose(0, 1, 3, 2, 4)
+    spectrum = spectrum.reshape(share, patches, 2, width)
+    coef = jnp.roll(coef[:, : 2 * ITERS], halves * lax.axis_index("freq"), axis=0)
+    coef = coef.reshape(patches, halves, ITERS, 2, fb).transpose(2, 0, 3, 1, 4)
+    return spectrum, coef.reshape(ITERS, patches, 2, width)
 
 
 def solution(mesh):

time: 150 us -> 120 us (0.80)
  local copies, waits for them, and re-layouts: 30.7 us -> 10.7 us
  Pallas kernels: 115 us -> 106 us
    convert_element_type x3 -> x0, local copies, waits for them, and re-layouts: 20 us -> none  [local(): spectrum = spectrum.reshape(share, patches, 2, halves * fb).astype(f32)]
    pallas_call x1, Pallas kernels: 115 us -> 101 us  [local(): pl.pallas_call(functools.partial(kernel, n_freq, n_trace), out_shape=(jax...]
    pallas_call x0 -> x1, Pallas kernels: none -> 5.08 us  [local(): pl.pallas_call(functools.partial(unpack, patches), out_shape=jax.ShapeDty...]
where the time goes in v2:
time: 120 us
  Pallas kernels  106 us (88%)
  local copies, waits for them, and re-layouts  10.7 us (9%)
  between operations  1.46 us (1%)
    pallas_call x1, Pallas kernels, local(): pl.pallas_call(functools.partial(kernel, n_freq, n_trace), out_shape=(jax...  101 us
    pallas_call x1, Pallas kernels, local(): pl.pallas_call(functools.partial(unpack, patches), out_shape=jax.ShapeDty...  5.08 us

profile of v2, /device:TPU:11, one launch (start us, length us, event | category | flops | bytes accessed | tf_op | source)
XLA Modules:
  0.0 119.8 jit_solution(10895252490429947140)
XLA Ops:
  0.6 0.0 copy-start
  0.7 1.3 %dynamic_slice.22 = s32[1]{0:T(128)} dynamic-slice(s32[4]{0:T(128)} %param.9, s32[]{:T(128)S(6)} %select_n.52), dynamic_slice_sizes={1} | dynamic-slice | bytes 12 | tf_op jit(solution)/shard_map/jit(dynamic_index_in_dim)/dynamic_slice | solution.py:304
  2.7 0.6 broadcast_in_dim.5.inv
  3.2 0.8 constant_dynamic-slice_fusion
  4.0 0.6 fusion.15
  4.7 0.9 constant_dynamic-slice_fusion.1
  5.6 0.1 fusion.11
  5.7 0.0 copy-done
  5.7 0.1 constant_dynamic-slice_fusion.2
  5.8 0.1 broadcast_multiply_fusion
  6.0 0.1 fusion.6
  6.0 0.3 copy.36
  6.3 0.2 copy.76
  6.6 0.9 pad_bitcast_fusion.1.cdt
  7.5 0.6 pad.11.clone.cd
  8.1 0.5 copy.35
  8.6 1.0 fusion.3
  9.6 1.2 pad_bitcast_fusion.wd
  10.7 0.6 copy.78
  11.3 1.3 %broadcast_in_dim.4.live = f32[2048,128]{1,0:T(8,128)} broadcast(f32[2048]{0:T(1024)S(1)} %fusion.15), dimensions={0} | broadcast | bytes 1056768 | tf_op jit(solution)/shard_map/broadcast_in_dim | solution.py:306
  12.7 100.5 %shard_map.77 = (bf16[8,512,256]{2,1,0:T(8,128)(2,1)}, f32[8,8,128]{2,1,0:T(8,128)}) custom-call(bf16[256,4096]{1,0:T(8,128)(2,1)} %bitcast.71, bf16[8,4096,256]{2,1,0:T(8,128)(2,1)} %constant.120.clone.table, bf16[4096,16]{1,0:T(8,128)(2,1)} %pad_bitcast_fusion.wd, bf16[16,2048]{1,0:T(8,128)(2,1)} %pad.11.clone.cd, bf16[2048,16]{1,0:T(8,128)(2,1)} %pad_bitcast_fusion.1.cdt, ...), custom_call_target="tpu_custom_call" | custom-call | tf_op jit(solution)/shard_map/pallas_call | solution.py:313
  113.2 0.8 slice.3
  114.0 0.6 copy.41
  114.7 5.1 %shard_map.78 = f32[8192,128]{1,0:T(8,128)} custom-call(bf16[8,512,256]{2,1,0:T(8,128)(2,1)} %get-tuple-element.4.recv), custom_call_target="tpu_custom_call" | custom-call | tf_op jit(solution)/shard_map/pallas_call | solution.py:338
  (4 shorter events, 0.1 us)
Async XLA Ops:
  0.6 5.1 %copy-start = (s32[4,4,4096]{2,1,0:T(4,128)S(1)}, s32[4,4,4096]{2,1,0:T(4,128)}, u32[]{:S(2)}) copy-start(s32[4,4,4096]{2,1,0:T(4,128)} %param.8) | copy-start | bytes 786436

commit v3 on v2

--- a/solution.py
+++ b/solution.py
@@ -13,10 +13,11 @@
 NF = 1024
 DIGIT = 32
 ITERS = 2
-PRE = 4
+PRE = 5
 MESH = pl.DeviceIdType.MESH
 
-SIN_ATOM = (6.2830558, -41.33121428, 81.36681487, -74.47800194, 32.78139554)
+SIN_ATOM = (6.27863545, -41.09373054, 77.93034795, -56.08638961)
+ROUNDER = 12582912.0
 COS_ATOM = (0.9999598, -19.73104175, 64.6734317, -82.40355228, 45.64655792)
 SIN_FINE = (6.28318527, -41.34169707, 81.60502462, -76.70155117, 42.01616576, -14.86861079, 3.19969338)
 COS_FINE = (0.99999999, -19.73920453, 64.93911899, -85.45016556, 60.16783179, -25.96831339, 6.52961042)
@@ -30,7 +31,7 @@
 
 
 def turn(x, sin_coefs, cos_coefs):
-    x = x - jnp.round(x)
+    x = x - ((x + ROUNDER) - ROUNDER)
     u = x * x
     return horner(u, cos_coefs), horner(u, sin_coefs) * x
 
@@ -45,7 +46,7 @@
     return pair.reshape(blocks, length, 2 * width).astype(ml_dtypes.bfloat16)
 
 
-def kernel(n_freq, n_trace, traces, table, wd, cd, cdt, kd, live, inv, recv, coef_out,
+def kernel(n_freq, n_trace, traces, table, wd, cd, cdt, kd, fold, recv, coef_out,
            tab, spec, spread, osc, res, atoms, obuf, coef_my,
            tab_sem, s_send, s_recv, s_loc, c_send, c_recv, o_send, o_recv, o_loc):
     halves = n_trace // n_freq
@@ -57,7 +58,7 @@
     fb = osc.shape[2]
     share = obuf.shape[1]
     n_buf = atoms.shape[0]
-    pre = n_buf - 1
+    pre = n_buf
 
     def table_copy(j):
         block = lax.rem(j + t, n_trace)
@@ -108,6 +109,10 @@
         @pl.when(jnp.logical_not(mine))
         def _():
             copy.start()
+
+    def live(k):
+        slot = lax.broadcasted_iota(jnp.int32, (slots, fb), 0) + k * slots
+        return jnp.where(slot.astype(jnp.float32) < fold[...], 1.0, 0.0)
 
     rows = min(256, share)
     lanes = 256
@@ -128,7 +133,7 @@
     @pl.loop(0, n_trace)
     def _(k):
         at = pl.ds(pl.multiple_of(k * slots, slots), slots)
-        on = live[at, :]
+        on = live(k)
         for it in range(ITERS):
             x = jnp.dot(cdt[at, :], kd[it], preferred_element_type=jnp.float32)
             cosine, sine = turn(x, SIN_FINE, COS_FINE)
@@ -166,7 +171,7 @@
     zero = jnp.zeros((8, fb), jnp.float32)
     sums = lax.fori_loop(0, n_trace, add_block, (zero,) * 6)
     p1r, p1i, p2r, p2i, gr, gi = (jnp.sum(a, axis=0, keepdims=True) for a in sums)
-    scale = inv[...]
+    scale = 1.0 / fold[...]
     a1r, a1i = p1r * scale, p1i * scale
     a2r = (p2r - (a1r * gr - a1i * gi)) * scale
     a2i = (p2i - (a1r * gi + a1i * gr)) * scale
@@ -193,7 +198,7 @@
     def _(k):
         at = pl.ds(pl.multiple_of(k * slots, slots), slots)
         under = pl.ds(pl.multiple_of(total + k * slots, slots), slots)
-        on = live[at, :]
+        on = live(k)
         x = spread[k].astype(jnp.float32)
         c1, s1, c2, s2 = (osc[n, at, :] for n in range(4))
         re = x[:, :fb] * on - (a1r * c1 - a1i * s1) - (a2r * c2 - a2i * s2)
@@ -212,6 +217,10 @@
     def _(i):
         buf = lax.rem(i, n_buf)
 
+        @pl.when(i >= pre)
+        def _():
+            make_atoms(i)
+
         @pl.loop(0, share // rows)
         def _(r):
             at = pl.ds(pl.multiple_of(r * rows, rows), rows)
@@ -220,10 +229,6 @@
         @pl.when(i < n_trace - 1)
         def _():
             out_copy(i).start()
-
-        @pl.when(i + pre < n_trace)
-        def _():
-            make_atoms(i + pre)
 
     own_out = pltpu.make_async_copy(obuf.at[n_trace - 1], recv.at[t], o_loc)
     own_out.start()
@@ -302,19 +307,17 @@
     picked = jnp.dot(waves, onehot, preferred_element_type=jnp.float32).astype(jnp.bfloat16)
     kd = picked.reshape(16, ITERS, fb).transpose(1, 0, 2)
     my_fold = lax.dynamic_index_in_dim(fold, patch, 0, keepdims=False)
-    live = (jnp.arange(total, dtype=jnp.int32) < my_fold).astype(jnp.float32)
-    live = jnp.broadcast_to(live[:, None], (total, fb))
-    inv = jnp.broadcast_to(1.0 / my_fold.astype(jnp.float32), (1, fb))
+    my_fold = jnp.broadcast_to(my_fold.astype(jnp.float32), (1, fb))
     vmem = pl.BlockSpec(memory_space=pltpu.VMEM)
     hbm = pl.BlockSpec(memory_space=pl.ANY)
     dma = pltpu.SemaphoreType.DMA
-    n_buf = min(PRE, n_trace - 1) + 1
+    n_buf = min(PRE, n_trace)
     bf16, f32 = jnp.bfloat16, jnp.float32
     recv, coef = pl.pallas_call(
         functools.partial(kernel, n_freq, n_trace),
         out_shape=(jax.ShapeDtypeStruct((n_trace, share, 2 * fb), bf16),
                    jax.ShapeDtypeStruct((n_trace, 8, fb), f32)),
-        in_specs=[vmem, hbm, vmem, vmem, vmem, vmem, vmem, vmem],
+        in_specs=[vmem, hbm, vmem, vmem, vmem, vmem, vmem],
         out_specs=(hbm, vmem),
         scratch_shapes=[
             pltpu.VMEM((2, length, 2 * fb), bf16),
@@ -330,7 +333,7 @@
         ],
         compiler_params=pltpu.CompilerParams(
             collective_id=0, has_side_effects=True, vmem_limit_bytes=58 * 1024 * 1024),
-    )(traces[0], table, waves.T, places, places.T, kd, live, inv)
+    )(traces[0], table, waves.T, places, places.T, kd, my_fold)
     width = halves * fb
     row = min(width, 128)
     step = min(share, 128)

time: 120 us -> 116 us (0.967)
  Pallas kernels: 106 us -> 104 us
  local copies, waits for them, and re-layouts: 10.7 us -> 9.39 us
    pallas_call x1, Pallas kernels: 101 us -> 98.5 us  [local(): pl.pallas_call(functools.partial(kernel, n_freq, n_trace), out_shape=(jax...]
    broadcast_in_dim x2 -> x1, local copies, waits for them, and re-layouts: 1.93 us -> 0.59 us  [local(): my_fold = jnp.broadcast_to(my_fold.astype(jnp.float32), (1, fb))]
where the time goes in v3:
time: 116 us
  Pallas kernels  104 us (90%)
  local copies, waits for them, and re-layouts  9.39 us (8%)
  between operations  1.41 us (1%)
    pallas_call x1, Pallas kernels, local(): pl.pallas_call(functools.partial(kernel, n_freq, n_trace), out_shape=(jax...  98.5 us
    pallas_call x1, Pallas kernels, local(): pl.pallas_call(functools.partial(unpack, patches), out_shape=jax.ShapeDty...  5.08 us

profile of v3, /device:TPU:11, one launch (start us, length us, event | category | flops | bytes accessed | tf_op | source)
XLA Modules:
  0.0 115.7 jit_solution(16301373147298097875)
XLA Ops:
  0.6 0.0 copy-start
  0.7 1.3 %dynamic_slice.22 = s32[1]{0:T(128)} dynamic-slice(s32[4]{0:T(128)} %param.9, s32[]{:T(128)S(6)} %select_n.52), dynamic_slice_sizes={1} | dynamic-slice | bytes 12 | tf_op jit(solution)/shard_map/jit(dynamic_index_in_dim)/dynamic_slice | solution.py:309
  2.6 0.6 broadcast_in_dim.4.fold
  3.2 0.8 constant_dynamic-slice_fusion
  4.0 0.9 constant_dynamic-slice_fusion.1
  4.9 0.1 fusion.11
  5.0 0.0 copy-done
  5.0 0.1 constant_dynamic-slice_fusion.2
  5.1 0.1 broadcast_multiply_fusion
  5.3 0.1 fusion.6
  5.3 0.3 copy.36
  5.6 0.2 copy.76
  5.9 0.9 pad_bitcast_fusion.1.cdt
  6.8 0.6 pad.11.clone.cd
  7.4 0.5 copy.35
  7.9 1.0 fusion.3
  8.9 1.2 %pad_bitcast_fusion.wd = bf16[4096,16]{1,0:T(8,128)(2,1)} fusion(bf16[12,4096]{0,1:T(8,128)(2,1)S(1)} %copy.35), kind=kLoop, calls=%fused_computation.6 | loop fusion | bytes 229376 | tf_op jit(solution)/shard_map/transpose | solution.py:336
  10.0 0.6 copy.78
  10.6 98.5 %shard_map.77 = (bf16[8,512,256]{2,1,0:T(8,128)(2,1)}, f32[8,8,128]{2,1,0:T(8,128)}) custom-call(bf16[256,4096]{1,0:T(8,128)(2,1)} %bitcast.71, bf16[8,4096,256]{2,1,0:T(8,128)(2,1)} %constant.118.clone.table, bf16[4096,16]{1,0:T(8,128)(2,1)} %pad_bitcast_fusion.wd, bf16[16,2048]{1,0:T(8,128)(2,1)} %pad.11.clone.cd, bf16[2048,16]{1,0:T(8,128)(2,1)} %pad_bitcast_fusion.1.cdt, ...), custom_call_target="tpu_custom_call" | custom-call | tf_op jit(solution)/shard_map/pallas_call | solution.py:316
  109.1 0.8 slice.3
  110.0 0.6 copy.41
  110.6 5.1 %shard_map.78 = f32[8192,128]{1,0:T(8,128)} custom-call(bf16[8,512,256]{2,1,0:T(8,128)(2,1)} %get-tuple-element.4.recv), custom_call_target="tpu_custom_call" | custom-call | tf_op jit(solution)/shard_map/pallas_call | solution.py:341
  (4 shorter events, 0.1 us)
Async XLA Ops:
  0.6 4.4 %copy-start = (s32[4,4,4096]{2,1,0:T(4,128)S(1)}, s32[4,4,4096]{2,1,0:T(4,128)}, u32[]{:S(2)}) copy-start(s32[4,4,4096]{2,1,0:T(4,128)} %param.8) | copy-start | bytes 786436
